TPU v7x, 512 devices: a whole 4x4x16 slice. The times are simulated.
512 devices in a mesh: blk: 128 (over x_lo, y, z), grp: 4 (over x_hi, core).
Axes of the slice: x: 4 (x_hi: 2, x_lo: 2; x = x_hi * 2 + x_lo), y: 4, z: 16, core: 2. Of those that a mesh axis runs over, the one named last changes fastest.
Arguments:
- view_a: bfloat16 [98304, 1024], P(('blk', 'grp')), may hold values from -1 to 1
- view_b: bfloat16 [98304, 1024], P(('blk', 'grp')), may hold values from -1 to 1
- positive: int32 [98304], P(('blk', 'grp')), may hold values from 0 to 98303, as said below
Outputs:
- row_loss: float32 [98304], P(('blk', 'grp'))
- grad_a: float32 [98304, 1024], P(('blk', 'grp'))
- grad_b: float32 [98304, 1024], P(('blk', 'grp'))
Inputs may be any that keep to these rules, and one draw needn't show every extreme that they name: Within each aligned block of 768 rows, positive is a permutation of that same block's row numbers.
All inputs are finite; a program needn't handle non-finite values.
Results may differ from a plain program's by a relative error of at most 0.0053.
Values may be sent and summed in bfloat16 or wider, within the bound.
A program may use at most 64 MiB of HBM per device.

v0:
```python
import jax
import jax.numpy as jnp
from jax import lax
from jax.sharding import PartitionSpec as P

SPAN = 2


inverse_temp = 20.0


def shifted(x, axis, by):
    devices = lax.axis_size(axis)
    return lax.ppermute(x, axis, [(i, (i + by) % devices) for i in range(devices)])


def merged(x, axis, combine):
    everything = jax.tree.map(lambda part: lax.all_gather(part, axis), x)
    initial = jax.tree.map(lambda part: part[0], everything)

    def step(k, so_far):
        return combine(so_far, jax.tree.map(lambda part: part[k], everything))

    return lax.fori_loop(1, lax.axis_size(axis), step, initial)


def tile_scores(left_rows, right_rows):
    return inverse_temp * lax.dot_general(
        left_rows, right_rows, (((1,), (1,)), ((), ())), preferred_element_type=jnp.float32
    )


def merge_stats(first, second):
    peak = jnp.maximum(first[0], second[0])
    total = first[1] * jnp.exp(first[0] - peak) + second[1] * jnp.exp(second[0] - peak)
    return (peak, total)


def body(view_a, view_b, positive):
    shard_rows = view_a.shape[0]
    width = view_a.shape[1]
    groups = lax.axis_size("grp")
    block_rows = shard_rows * groups
    grp_index = lax.axis_index("grp")
    blk_index = lax.axis_index("blk")
    query_block, key_block = (
        lax.all_gather(view_a, "grp", axis=0, tiled=True),
        lax.all_gather(view_b, "grp", axis=0, tiled=True),
    )
    block_pos = lax.all_gather(positive, "grp", axis=0, tiled=True)
    block_start = blk_index * block_rows
    offsets = list(range(-SPAN, SPAN + 1))
    pieces = {0: view_b}
    for sign in (1, -1):
        current = view_b
        for hop in range(1, SPAN + 1):
            current = shifted(current, "blk", -sign)
            pieces[sign * hop] = current
    window_keys = jnp.concatenate([pieces[s] for s in offsets], axis=0)
    scores = tile_scores(query_block, window_keys)
    peak = jnp.max(scores, axis=1)
    total = jnp.sum(jnp.exp(scores - peak[:, None]), axis=1)
    peak, total = merged((peak, total), "grp", merge_stats)
    lse_block = peak + jnp.log(total)
    lse_own = lax.dynamic_slice_in_dim(lse_block, grp_index * shard_rows, shard_rows, 0)
    own_local = positive - block_start
    own_match = jnp.take(key_block, own_local, axis=0).astype(jnp.float32)
    matched = inverse_temp * jnp.sum(view_a.astype(jnp.float32) * own_match, axis=1)
    row_loss = lse_own - matched
    weights = jnp.exp(scores - lse_block[:, None]).astype(jnp.bfloat16)
    query_part = jnp.dot(weights, window_keys, preferred_element_type=jnp.float32)
    query_rows = lax.psum_scatter(query_part, "grp", scatter_dimension=0, tiled=True)
    grad_a = inverse_temp * (query_rows - own_match)
    key_part = lax.dot_general(
        weights, query_block, (((0,), (0,)), ((), ())), preferred_element_type=jnp.float32
    )
    terms = {}
    for place, step_off in enumerate(offsets):
        terms[step_off] = key_part[place * shard_rows : (place + 1) * shard_rows]
    home = terms[0]
    for sign in (1, -1):
        carried = jnp.zeros((shard_rows, width), jnp.float32)
        for hop in range(SPAN, 0, -1):
            carried = shifted(carried + terms[sign * hop], "blk", sign)
        home = home + carried
    key_global = block_start + grp_index * shard_rows + jnp.arange(shard_rows, dtype=jnp.int32)
    hits = (key_global[:, None] == block_pos[None, :]).astype(jnp.bfloat16)
    matched_rows = jnp.dot(hits, query_block, preferred_element_type=jnp.float32)
    grad_b = inverse_temp * (home - matched_rows)
    return (row_loss, grad_a, grad_b)


def solution(mesh):
    in_specs = (P(("blk", "grp"), None), P(("blk", "grp"), None), P(("blk", "grp")))
    out_specs = (P(("blk", "grp")), P(("blk", "grp"), None), P(("blk", "grp"), None))
    return jax.shard_map(body, mesh=mesh, in_specs=in_specs, out_specs=out_specs, check_vma=False)
```

profile of v0, /device:TPU:25, one launch (start us, length us, event | category | flops | bytes accessed | tf_op | source)
XLA Modules:
  0.0 166.3 jit_solution(14209084635062048930)
XLA Ops:
  8.0 3.5 %collective-permute-start = (bf16[192,1024]{1,0:T(8,128)(2,1)}, bf16[192,1024]{1,0:T(8,128)(2,1)S(1)}, u32[]{:S(2)}, u32[]{:S(2)}) collective-permute-start(bf16[192,1024]{1,0:T(8,128)(2,1)} %param.6), channel_id=1, source_target_pairs={{0,4},{4,8},{8,12},{12,16},{16,20},{20,24},{24,28},{28,32},{32,36}... | collective-permute-start | bytes 1179656 | tf_op jit(solution)/shard_map/ppermute | solution.py:14
  11.5 9.7 %collective-permute-start.2 = (bf16[192,1024]{1,0:T(8,128)(2,1)}, bf16[192,1024]{1,0:T(8,128)(2,1)S(1)}, u32[]{:S(2)}, u32[]{:S(2)}) collective-permute-start(bf16[192,1024]{1,0:T(8,128)(2,1)} %param.6), channel_id=1, source_target_pairs={{0,508},{4,0},{8,4},{12,8},{16,12},{20,16},{24,20},{28,24},{32,28}... | collective-permute-start | bytes 1179656 | tf_op jit(solution)/shard_map/ppermute | solution.py:14
  21.2 7.1 %collective-permute-done = bf16[192,1024]{1,0:T(8,128)(2,1)S(1)} collective-permute-done((bf16[192,1024]{1,0:T(8,128)(2,1)}, bf16[192,1024]{1,0:T(8,128)(2,1)S(1)}, u32[]{:S(2)}, u32[]{:S(2)}) %collective-permute-start) | collective-permute-done | bytes 393248 | tf_op jit(solution)/shard_map/ppermute | solution.py:14
  28.3 1.9 %collective-permute-start.1 = (bf16[192,1024]{1,0:T(8,128)(2,1)S(1)}, bf16[192,1024]{1,0:T(8,128)(2,1)S(1)}, u32[]{:S(2)}, u32[]{:S(2)}) collective-permute-start(bf16[192,1024]{1,0:T(8,128)(2,1)S(1)} %collective-permute-done), channel_id=1, source_target_pairs={{0,4},{4,8},{8,12},{12,16},{16,20},{20,24},{24,28},{28,32},{32,36}... | collective-permute-start | bytes 1179656 | tf_op jit(solution)/shard_map/ppermute | solution.py:14
  30.3 5.5 %collective-permute-start.3 = (bf16[192,1024]{1,0:T(8,128)(2,1)S(1)}, bf16[192,1024]{1,0:T(8,128)(2,1)S(1)}, u32[]{:S(2)}, u32[]{:S(2)}) collective-permute-start(bf16[192,1024]{1,0:T(8,128)(2,1)S(1)} %collective-permute-done.2), channel_id=1, source_target_pairs={{0,508},{4,0},{8,4},{12,8},{16,12},{20,16},{24,20},{28,24},{32,28}... | collective-permute-start | bytes 1179656 | tf_op jit(solution)/shard_map/ppermute | solution.py:14
  35.8 6.0 %collective-permute-done.1 = bf16[192,1024]{1,0:T(8,128)(2,1)S(1)} collective-permute-done((bf16[192,1024]{1,0:T(8,128)(2,1)S(1)}, bf16[192,1024]{1,0:T(8,128)(2,1)S(1)}, u32[]{:S(2)}, u32[]{:S(2)}) %collective-permute-start.1) | collective-permute-done | bytes 393248 | tf_op jit(solution)/shard_map/ppermute | solution.py:14
  45.7 8.9 %all-gather.7.cloned.1.call-done = bf16[768,1024]{1,0:T(8,128)(2,1)} async-done(((bf16[192,1024]{1,0:T(8,128)(2,1)}), bf16[768,1024]{1,0:T(8,128)(2,1)}) %all-gather.7.cloned.1.call-update) | async-done | bytes 1572880 | tf_op jit(solution)/shard_map/all_gather | solution.py:47
  54.5 3.7 %multiply_reduce_fusion = (f32[768]{0:T(1024)S(1)}, f32[960,768]{1,0:T(8,128)S(1)}) fusion(bf16[960,1024]{1,0:T(8,128)(2,1)} %constant_dynamic-update-slice_fusion, bf16[768,1024]{1,0:T(8,128)(2,1)} %all-gather.7.cloned.1.call-done), kind=kOutput, calls=%fused_computation.6 | convolution fusion | flops 1511423232 | bytes 6491136 | tf_op jit(solution)/shard_map/dot_general | solution.py:28
  58.8 6.7 %all-gather.2 = f32[4,1,768]{2,1,0:T(1,128)S(1)} all-gather(f32[1,1,768]{2,1,0:T(1,128)S(1)} %reshape.36), channel_id=2, replica_groups=mesh['blk'=128,'grp'=4] {'grp'}, dimensions={0}, use_global_device_ids=true | all-gather | bytes 15360 | tf_op jit(solution)/shard_map/all_gather | solution.py:18
  65.6 6.7 %all-gather.3 = f32[4,1,768]{2,1,0:T(1,128)S(1)} all-gather(f32[1,1,768]{2,1,0:T(1,128)S(1)} %reshape.38), channel_id=3, replica_groups=mesh['blk'=128,'grp'=4] {'grp'}, dimensions={0}, use_global_device_ids=true | all-gather | bytes 15360 | tf_op jit(solution)/shard_map/all_gather | solution.py:18
  72.5 5.1 %fusion.10 = f32[768,1024]{1,0:T(8,128)} fusion(bf16[960,1024]{1,0:T(8,128)(2,1)} %constant_dynamic-update-slice_fusion, f32[960,768]{1,0:T(8,128)S(1)} %get-tuple-element.161, f32[768]{0:T(1024)S(1)} %log_add_fusion), kind=kOutput, calls=%fused_computation.23 | convolution fusion | flops 1512161280 | bytes 8064000 | tf_op jit(solution)/shard_map/dot_general | solution.py:71
  77.7 3.1 %fusion.9 = f32[960,1024]{1,0:T(8,128)S(1)} fusion(bf16[768,1024]{1,0:T(8,128)(2,1)} %all-gather.7.cloned.1.call-done, f32[960,768]{1,0:T(8,128)S(1)} %get-tuple-element.161, f32[768]{0:T(1024)S(1)} %log_add_fusion), kind=kOutput, calls=%fused_computation.22 | convolution fusion | flops 1512161280 | bytes 8457216 | tf_op jit(solution)/shard_map/dot_general | solution.py:74
  81.0 1.9 %collective-permute-start.4 = (f32[192,1024]{1,0:T(8,128)S(1)}, f32[192,1024]{1,0:T(8,128)S(1)}, u32[]{:S(2)}, u32[]{:S(2)}) collective-permute-start(f32[192,1024]{1,0:T(8,128)S(1)} %get-tuple-element.156), channel_id=1, source_target_pairs={{0,4},{4,8},{8,12},{12,16},{16,20},{20,24},{24,28},{28,32},{32,36}... | collective-permute-start | bytes 2359304 | tf_op jit(solution)/shard_map/ppermute | solution.py:14
  82.9 5.5 %collective-permute-start.6 = (f32[192,1024]{1,0:T(8,128)S(1)}, f32[192,1024]{1,0:T(8,128)S(1)}, u32[]{:S(2)}, u32[]{:S(2)}) collective-permute-start(f32[192,1024]{1,0:T(8,128)S(1)} %get-tuple-element.157), channel_id=1, source_target_pairs={{0,508},{4,0},{8,4},{12,8},{16,12},{20,16},{24,20},{28,24},{32,28}... | collective-permute-start | bytes 2359304 | tf_op jit(solution)/shard_map/ppermute | solution.py:14
  88.4 15.5 %collective-permute-done.4 = f32[192,1024]{1,0:T(8,128)S(1)} collective-permute-done((f32[192,1024]{1,0:T(8,128)S(1)}, f32[192,1024]{1,0:T(8,128)S(1)}, u32[]{:S(2)}, u32[]{:S(2)}) %collective-permute-start.4) | collective-permute-done | bytes 786464 | tf_op jit(solution)/shard_map/ppermute | solution.py:14
  105.1 6.4 %collective-permute-start.7 = (f32[192,1024]{1,0:T(8,128)S(1)}, f32[192,1024]{1,0:T(8,128)}, u32[]{:S(2)}, u32[]{:S(2)}) collective-permute-start(f32[192,1024]{1,0:T(8,128)S(1)} %get-tuple-element.155), channel_id=1, source_target_pairs={{0,508},{4,0},{8,4},{12,8},{16,12},{20,16},{24,20},{28,24},{32,28}... | collective-permute-start | bytes 2359304 | tf_op jit(solution)/shard_map/ppermute | solution.py:14
  111.5 1.9 %collective-permute-start.5 = (f32[192,1024]{1,0:T(8,128)S(1)}, f32[192,1024]{1,0:T(8,128)}, u32[]{:S(2)}, u32[]{:S(2)}) collective-permute-start(f32[192,1024]{1,0:T(8,128)S(1)} %get-tuple-element.154), channel_id=1, source_target_pairs={{0,4},{4,8},{8,12},{12,16},{16,20},{20,24},{24,28},{28,32},{32,36}... | collective-permute-start | bytes 2359304 | tf_op jit(solution)/shard_map/ppermute | solution.py:14
  115.6 5.0 %all-reduce = s32[768]{0:T(1024)S(1)} all-reduce(s32[768]{0:T(1024)S(1)} %dynamic-update-slice), channel_id=1, replica_groups=mesh['blk'=128,'grp'=4] {'grp'}, use_global_device_ids=true, to_apply=%add | all-reduce | flops 768 | bytes 6144
  121.3 2.9 %gather_fusion = bf16[192,1024]{1,0:T(8,128)(2,1)S(1)} fusion(bf16[768,1024]{1,0:T(8,128)(2,1)} %all-gather.9.cloned.1.call-done, s32[1024]{0:T(1024)S(1)} %pad_clamp_fusion), kind=kCustom, calls=%fused_computation | custom fusion | bytes 787200 | tf_op jit(solution)/shard_map/jit(_take)/gather | solution.py:67
  125.4 1.6 collective-permute-done.7
  127.0 6.1 %collective-permute-done.5 = f32[192,1024]{1,0:T(8,128)} collective-permute-done((f32[192,1024]{1,0:T(8,128)S(1)}, f32[192,1024]{1,0:T(8,128)}, u32[]{:S(2)}, u32[]{:S(2)}) %collective-permute-start.5) | collective-permute-done | bytes 786464 | tf_op jit(solution)/shard_map/ppermute | solution.py:14
  133.0 2.8 %fusion.4 = f32[192,1024]{1,0:T(8,128)} fusion(f32[192,1024]{1,0:T(8,128)S(1)} %fusion.5, f32[192,1024]{1,0:T(8,128)} %collective-permute-done.7, f32[192,1024]{1,0:T(8,128)} %collective-permute-done.5, f32[960,1024]{1,0:T(8,128)} %copy-done), kind=kLoop, calls=%fused_computation.16 | loop fusion | flops 786432 | bytes 3932160 | tf_op jit(solution)/shard_map/mul | solution.py:89
  135.8 21.0 %reduce-scatter.2.cloned.1.call-done = f32[192,1024]{1,0:T(8,128)} async-done(((f32[768,1024]{1,0:T(8,128)}), f32[192,1024]{1,0:T(8,128)}) %reduce-scatter.2.cloned.1.call-update) | async-done | bytes 786448 | tf_op jit(solution)/shard_map/reduce_scatter | solution.py:72
  156.8 2.3 %fusion.1 = (f32[192,1024]{1,0:T(8,128)}, f32[192]{0:T(256)S(1)}) fusion(f32[192,1024]{1,0:T(8,128)} %reduce-scatter.2.cloned.1.call-done, bf16[192,1024]{1,0:T(8,128)(2,1)S(1)} %gather_fusion, pred[192]{0:T(512)(128)(4,1)S(1)} %get-tuple-element.150, bf16[192,1024]{1,0:T(8,128)(2,1)S(1)} %copy-done.2), kind=kLoop, calls=%fused_computation.10 | loop fusion | flops 1376064 | bytes 2360256 | tf_op jit(solution)/shard_map/mul | solution.py:73
  (50 shorter events, 10.9 us)
Async XLA Ops:
  7.2 36.2 %copy-start.1 = (bf16[192,1024]{1,0:T(8,128)(2,1)S(1)}, bf16[192,1024]{1,0:T(8,128)(2,1)}, u32[]{:S(2)}) copy-start(bf16[192,1024]{1,0:T(8,128)(2,1)} %param.6) | copy-start | bytes 1179652
  7.2 47.4 %all-gather.7.cloned.1.call-start = ((), (), s32[]{:S(2)}) async-start(), calls=%async_computation.1 | async-start | bytes 1966080 | tf_op jit(solution)/shard_map/all_gather | solution.py:47
  7.9 113.3 %all-gather.9.cloned.1.call-start = ((), (), s32[]{:S(2)}) async-start(), calls=%async_computation.2 | async-start | bytes 1966080 | tf_op jit(solution)/shard_map/all_gather | solution.py:48
  8.0 20.3 %collective-permute-start = (bf16[192,1024]{1,0:T(8,128)(2,1)}, bf16[192,1024]{1,0:T(8,128)(2,1)S(1)}, u32[]{:S(2)}, u32[]{:S(2)}) collective-permute-start(bf16[192,1024]{1,0:T(8,128)(2,1)} %param.6), channel_id=1, source_target_pairs={{0,4},{4,8},{8,12},{12,16},{16,20},{20,24},{24,28},{28,32},{32,36}... | collective-permute-start | bytes 1179656 | tf_op jit(solution)/shard_map/ppermute | solution.py:14
  11.5 18.8 %collective-permute-start.2 = (bf16[192,1024]{1,0:T(8,128)(2,1)}, bf16[192,1024]{1,0:T(8,128)(2,1)S(1)}, u32[]{:S(2)}, u32[]{:S(2)}) collective-permute-start(bf16[192,1024]{1,0:T(8,128)(2,1)} %param.6), channel_id=1, source_target_pairs={{0,508},{4,0},{8,4},{12,8},{16,12},{20,16},{24,20},{28,24},{32,28}... | collective-permute-start | bytes 1179656 | tf_op jit(solution)/shard_map/ppermute | solution.py:14
  28.3 13.5 %collective-permute-start.1 = (bf16[192,1024]{1,0:T(8,128)(2,1)S(1)}, bf16[192,1024]{1,0:T(8,128)(2,1)S(1)}, u32[]{:S(2)}, u32[]{:S(2)}) collective-permute-start(bf16[192,1024]{1,0:T(8,128)(2,1)S(1)} %collective-permute-done), channel_id=1, source_target_pairs={{0,4},{4,8},{8,12},{12,16},{16,20},{20,24},{24,28},{28,32},{32,36}... | collective-permute-start | bytes 1179656 | tf_op jit(solution)/shard_map/ppermute | solution.py:14
  30.2 126.6 %reduce-scatter.2.cloned.1.call-start = ((), (), s32[]{:S(2)}) async-start(), calls=%async_computation.3 | async-start | bytes 3932160 | tf_op jit(solution)/shard_map/reduce_scatter | solution.py:72
  30.3 14.6 %collective-permute-start.3 = (bf16[192,1024]{1,0:T(8,128)(2,1)S(1)}, bf16[192,1024]{1,0:T(8,128)(2,1)S(1)}, u32[]{:S(2)}, u32[]{:S(2)}) collective-permute-start(bf16[192,1024]{1,0:T(8,128)(2,1)S(1)} %collective-permute-done.2), channel_id=1, source_target_pairs={{0,508},{4,0},{8,4},{12,8},{16,12},{20,16},{24,20},{28,24},{32,28}... | collective-permute-start | bytes 1179656 | tf_op jit(solution)/shard_map/ppermute | solution.py:14
  80.8 24.3 %copy-start = (f32[960,1024]{1,0:T(8,128)}, f32[960,1024]{1,0:T(8,128)S(1)}, u32[]{:S(2)}) copy-start(f32[960,1024]{1,0:T(8,128)S(1)} %fusion.9) | copy-start | bytes 11796484
  81.0 23.0 %collective-permute-start.4 = (f32[192,1024]{1,0:T(8,128)S(1)}, f32[192,1024]{1,0:T(8,128)S(1)}, u32[]{:S(2)}, u32[]{:S(2)}) collective-permute-start(f32[192,1024]{1,0:T(8,128)S(1)} %get-tuple-element.156), channel_id=1, source_target_pairs={{0,4},{4,8},{8,12},{12,16},{16,20},{20,24},{24,28},{28,32},{32,36}... | collective-permute-start | bytes 2359304 | tf_op jit(solution)/shard_map/ppermute | solution.py:14
  82.9 32.5 %copy-start.4 = (s32[192]{0:T(256)S(1)}, s32[192]{0:T(256)}, u32[]{:S(2)}) copy-start(s32[192]{0:T(256)} %param.7) | copy-start | bytes 2308
  82.9 21.9 %collective-permute-start.6 = (f32[192,1024]{1,0:T(8,128)S(1)}, f32[192,1024]{1,0:T(8,128)S(1)}, u32[]{:S(2)}, u32[]{:S(2)}) collective-permute-start(f32[192,1024]{1,0:T(8,128)S(1)} %get-tuple-element.157), channel_id=1, source_target_pairs={{0,508},{4,0},{8,4},{12,8},{16,12},{20,16},{24,20},{28,24},{32,28}... | collective-permute-start | bytes 2359304 | tf_op jit(solution)/shard_map/ppermute | solution.py:14
  105.1 19.1 %copy-start.3 = (bf16[768,1024]{1,0:T(8,128)(2,1)S(1)}, bf16[768,1024]{1,0:T(8,128)(2,1)}, u32[]{:S(2)}) copy-start(bf16[768,1024]{1,0:T(8,128)(2,1)} %all-gather.7.cloned.1.call-done) | copy-start | bytes 4718596
  105.1 21.8 %collective-permute-start.7 = (f32[192,1024]{1,0:T(8,128)S(1)}, f32[192,1024]{1,0:T(8,128)}, u32[]{:S(2)}, u32[]{:S(2)}) collective-permute-start(f32[192,1024]{1,0:T(8,128)S(1)} %get-tuple-element.155), channel_id=1, source_target_pairs={{0,508},{4,0},{8,4},{12,8},{16,12},{20,16},{24,20},{28,24},{32,28}... | collective-permute-start | bytes 2359304 | tf_op jit(solution)/shard_map/ppermute | solution.py:14
  111.5 21.5 %collective-permute-start.5 = (f32[192,1024]{1,0:T(8,128)S(1)}, f32[192,1024]{1,0:T(8,128)}, u32[]{:S(2)}, u32[]{:S(2)}) collective-permute-start(f32[192,1024]{1,0:T(8,128)S(1)} %get-tuple-element.154), channel_id=1, source_target_pairs={{0,4},{4,8},{8,12},{12,16},{16,20},{20,24},{24,28},{28,32},{32,36}... | collective-permute-start | bytes 2359304 | tf_op jit(solution)/shard_map/ppermute | solution.py:14
  125.4 31.4 %copy-start.2 = (bf16[192,1024]{1,0:T(8,128)(2,1)S(1)}, bf16[192,1024]{1,0:T(8,128)(2,1)}, u32[]{:S(2)}) copy-start(bf16[192,1024]{1,0:T(8,128)(2,1)} %param.5) | copy-start | bytes 1179652
Sparse Core Ops, SparseCore 0:
  10.1 44.3 all-gather.6
  56.6 22.5 all-gather.8
  82.3 74.5 reduce-scatter.1
where the time goes:
time: 167 us; the launch traced here: 166 us
  waiting for transfers between devices  67.8 us (41%)
  starting transfers between devices  36.4 us (22%)
  blocking collectives  18.5 us (11%)
  between operations  14.6 us (9%)
  matrix products  13.2 us (8%)
  local copies, waits for them, and re-layouts  8.64 us (5%)
  other arithmetic  7.14 us (4%)
    ppermute x8, waiting for transfers between devices, shifted(): lax.ppermute(x, axis, [(i, (i + by) % devices) for i in range(devices)])  37.1 us
    ppermute x8, starting transfers between devices, shifted(): lax.ppermute(x, axis, [(i, (i + by) % devices) for i in range(devices)])  36.3 us
    reduce_scatter x1, waiting for transfers between devices, body(): lax.psum_scatter(query_part, 'grp', scatter_dimension=0, tiled=True)  21 us
    all_gather x2, blocking collectives, merged(): everything = jax.tree.map(lambda part: lax.all_gather(part, axis), x)  13.4 us
    all_gather x1, waiting for transfers between devices, body(): lax.all_gather(view_a, 'grp', axis=0, tiled=True)  8.86 us
    dot_general x1, matrix products, body(): jnp.dot(weights, window_keys, preferred_element_type=jnp.float32)  5.11 us
    unnamed x1, blocking collectives  5.03 us
    unnamed x21, local copies, waits for them, and re-layouts  4.68 us
  transfers between devices with their start and end apart: 11, of which 8 were waited for; matrix products, arithmetic and copies ran while one was open for 16% of the time, Pallas kernels for 0%

commit v1 on v0

v1 whole, which is shorter than its diff:
```python
import functools

import jax
import jax.numpy as jnp
from jax import lax
from jax.experimental import pallas as pl
from jax.experimental.pallas import tpu as pltpu
from jax.sharding import PartitionSpec as P

SPAN = 2
WINDOW = 2 * SPAN + 1
GROUPS = 4
CHUNKS = 2
inverse_temp = 20.0
MESH = pl.DeviceIdType.MESH
TOP = 32766.0


def encode(x):
    peak = jnp.max(jnp.abs(x), axis=0, keepdims=True)
    alive = peak > 1e-30
    scale = jnp.where(alive, TOP / jnp.where(alive, peak, 1.0), 0.0)
    codes = jnp.round(x * scale).astype(jnp.int32).astype(jnp.int16)
    return codes, jnp.where(alive, peak * (1.0 / TOP), 0.0)


def decode(codes, step):
    return codes.astype(jnp.int32).astype(jnp.float32) * step


def kernel(
    a_in, b_in, pos_in, loss_out, grad_a_out, grad_b_out,
    queries, keys, pos_buf, stat_buf, scores, weights, hits_buf,
    home, side, code1_out, step1_out, code1_in, step1_in, code2_out, step2_out, code2_in, step2_in,
    part, sib_in, codex_out, stepx_out, codex_in, stepx_in,
    load_sem, b_send, b_recv, a_send, a_recv, p_send, p_recv, s_send, s_recv,
    c_send, c_recv, t_send, t_recv, d_send, d_recv, x_send, x_recv,
):
    rows, width = a_in.shape
    block = rows * GROUPS
    cut = rows // CHUNKS
    blk = lax.axis_index("blk")
    grp = lax.axis_index("grp")
    blocks = lax.axis_size("blk")
    right = lax.rem(blk + 1, blocks)
    left = lax.rem(blk + blocks - 1, blocks)
    sib = grp + 1 - 2 * lax.rem(grp, 2)
    par = lax.rem(grp + 2, GROUPS)
    dia = lax.rem(sib + 2, GROUPS)
    ways = (right, left)
    peers = (sib, par, dia)

    def remote(src, dst, send, recv, to_blk, to_grp):
        return pltpu.make_async_remote_copy(
            src_ref=src, dst_ref=dst, send_sem=send, recv_sem=recv,
            device_id=(to_blk, to_grp), device_id_type=MESH,
        )

    load_b = pltpu.make_async_copy(b_in, keys.at[SPAN], load_sem.at[0])
    load_a = pltpu.make_async_copy(a_in, queries.at[grp], load_sem.at[1])
    load_b.start()
    load_a.start()
    pos_buf[grp] = jnp.zeros(pos_buf.shape[1:], jnp.int32)
    pos_buf[grp, 0:1, 0:rows] = pos_in[...] - blk * block

    barrier = pltpu.get_barrier_semaphore()
    for way in ways:
        pl.semaphore_signal(barrier, inc=1, device_id=(way, grp), device_id_type=MESH)
    for peer in peers:
        pl.semaphore_signal(barrier, inc=1, device_id=(blk, peer), device_id_type=MESH)
    pl.semaphore_wait(barrier, 5)
    load_b.wait()
    load_a.wait()

    def key_copy(hop, d, c):
        part_rows = pl.ds(c * cut, cut)
        src = SPAN if hop == 0 else (SPAN - 1, SPAN + 1)[d]
        dst = ((SPAN - 1, SPAN + 1), (SPAN - 2, SPAN + 2))[hop][d]
        return remote(
            keys.at[src, part_rows], keys.at[dst, part_rows],
            b_send.at[hop, d, c], b_recv.at[hop, d, c], ways[d], grp,
        )

    key_copies = {(h, d, c): key_copy(h, d, c) for h in range(2) for d in range(2) for c in range(CHUNKS)}
    for c in range(CHUNKS):
        for d in range(2):
            key_copies[0, d, c].start()
        if c == 0:
            to_par = remote(queries.at[grp], queries.at[grp], a_send.at[1], a_recv.at[1], blk, par)
            to_par.start()
            to_sib = remote(queries.at[grp], queries.at[grp], a_send.at[0], a_recv.at[0], blk, sib)
            to_sib.start()
    pos_copies = [
        remote(pos_buf.at[grp], pos_buf.at[grp], p_send.at[i], p_recv.at[i], blk, peer)
        for i, peer in enumerate(peers)
    ]
    for copy in pos_copies:
        copy.start()
    for c in range(CHUNKS):
        for d in range(2):
            key_copies[0, d, c].wait_recv()
            key_copies[1, d, c].start()
    to_par.wait_recv()
    onward = remote(queries.at[par], queries.at[par], a_send.at[2], a_recv.at[2], blk, sib)
    onward.start()
    to_sib.wait_recv()
    onward.wait_recv()
    for copy in pos_copies:
        copy.wait_recv()

    every_query = queries[...].reshape(block, width)

    def score(s, lo, size):
        scores[s, lo : lo + size, :] = inverse_temp * lax.dot_general(
            keys[s, lo : lo + size, :], every_query, (((1,), (1,)), ((), ())),
            preferred_element_type=jnp.float32,
        )

    for s in (SPAN, SPAN - 1, SPAN + 1):
        score(s, 0, rows)
    place = jnp.concatenate([pos_buf[t, 0:1, 0:rows] for t in range(GROUPS)], axis=1)
    own_rows = lax.broadcasted_iota(jnp.int32, (rows, block), 0) + grp * rows
    hits = own_rows == place
    hits_buf[...] = jnp.where(hits, 1.0, 0.0).astype(jnp.bfloat16)
    matched = jnp.sum(jnp.where(hits, scores[SPAN], 0.0), axis=0, keepdims=True)
    near = [SPAN, SPAN - 1, SPAN + 1]
    far = [SPAN - 2, SPAN + 2]
    peak3 = functools.reduce(jnp.maximum, [jnp.max(scores[s], axis=0, keepdims=True) for s in near])
    total3 = sum(jnp.sum(jnp.exp(scores[s] - peak3), axis=0, keepdims=True) for s in near)
    for c in range(CHUNKS):
        for d in range(2):
            key_copies[1, d, c].wait_recv()
            score(far[d], c * cut, cut)
    peak = functools.reduce(jnp.maximum, [peak3] + [jnp.max(scores[s], axis=0, keepdims=True) for s in far])
    total = total3 * jnp.exp(peak3 - peak)
    total = total + sum(jnp.sum(jnp.exp(scores[s] - peak), axis=0, keepdims=True) for s in far)

    stat_buf[grp] = jnp.zeros(stat_buf.shape[1:], jnp.float32)
    stat_buf[grp, 0:1, :] = peak
    stat_buf[grp, 1:2, :] = total
    stat_buf[grp, 2:3, :] = matched
    stat_copies = [
        remote(stat_buf.at[grp], stat_buf.at[grp], s_send.at[i], s_recv.at[i], blk, peer)
        for i, peer in enumerate(peers)
    ]
    for copy in stat_copies:
        copy.start()
    for copy in stat_copies:
        copy.wait_recv()
    peaks = [stat_buf[t, 0:1, :] for t in range(GROUPS)]
    peak = functools.reduce(jnp.maximum, peaks)
    total = sum(stat_buf[t, 1:2, :] * jnp.exp(peaks[t] - peak) for t in range(GROUPS))
    lse = peak + jnp.log(total)
    loss_out[...] = lse - sum(stat_buf[t, 2:3, :] for t in range(GROUPS))

    def weigh(s, lo, size):
        weights[s, lo : lo + size, :] = jnp.exp(scores[s, lo : lo + size, :] - lse).astype(jnp.bfloat16)

    def term(s, lo, size):
        weigh(s, lo, size)
        return jnp.dot(weights[s, lo : lo + size, :], every_query, preferred_element_type=jnp.float32)

    def code_copies(hop, d, c):
        codes = (code1_out, code2_out)[hop], (code1_in, code2_in)[hop]
        steps = (step1_out, step2_out)[hop], (step1_in, step2_in)[hop]
        part_rows = pl.ds(c * cut, cut)
        return (
            remote(codes[0].at[d, part_rows], codes[1].at[d, part_rows], c_send.at[hop, d, c], c_recv.at[hop, d, c], ways[d], grp),
            remote(steps[0].at[d, c], steps[1].at[d, c], t_send.at[hop, d, c], t_recv.at[hop, d, c], ways[d], grp),
        )

    back = {(h, d, c): code_copies(h, d, c) for h in range(2) for d in range(2) for c in range(CHUNKS)}

    def send_back(hop, d, c, value):
        codes_out, steps_out = ((code1_out, step1_out), (code2_out, step2_out))[hop]
        codes, step = encode(value)
        codes_out[d, c * cut : (c + 1) * cut, :] = codes
        steps_out[d, c] = step
        for copy in back[hop, d, c]:
            copy.start()

    def received(hop, d, c):
        for copy in back[hop, d, c]:
            copy.wait_recv()
        codes_in, steps_in = ((code1_in, step1_in), (code2_in, step2_in))[hop]
        return decode(codes_in[d, c * cut : (c + 1) * cut, :], steps_in[d, c])

    to_far, to_near = (SPAN + 2, SPAN - 2), (SPAN + 1, SPAN - 1)
    for c in range(CHUNKS):
        for d in range(2):
            send_back(0, d, c, term(to_far[d], c * cut, cut))
    for d in range(2):
        side[d] = term(to_near[d], 0, rows)
    home[...] = term(SPAN, 0, rows) - jnp.dot(hits_buf[...], every_query, preferred_element_type=jnp.float32)

    every_weight = weights[...].reshape(WINDOW * rows, block)
    window = keys[...].reshape(WINDOW * rows, width)
    across = (((0,), (0,)), ((), ()))
    query_part = lax.dot_general(every_weight, window, across, preferred_element_type=jnp.float32)
    query_part = query_part - lax.dot_general(
        hits_buf[...], keys[SPAN], across, preferred_element_type=jnp.float32
    )
    part[...] = query_part.reshape(GROUPS, rows, width)
    sib_copies = [
        remote(part.at[t], sib_in.at[i], d_send.at[i], d_recv.at[i], blk, sib)
        for i, t in ((1, dia), (0, sib))
    ]
    for copy in sib_copies:
        copy.start()

    for d in range(2):
        send_back(1, d, 0, side[d, 0:cut, :] + received(0, d, 0))
    for copy in sib_copies:
        copy.wait_recv()
    codes, step = encode(part[par] + sib_in[1])
    codex_out[...] = codes
    stepx_out[...] = step
    x_copies = (
        remote(codex_out, codex_in, x_send.at[0], x_recv.at[0], blk, par),
        remote(stepx_out, stepx_in, x_send.at[1], x_recv.at[1], blk, par),
    )
    for copy in x_copies:
        copy.start()
    for c in range(1, CHUNKS):
        for d in range(2):
            lo = c * cut
            send_back(1, d, c, side[d, lo : lo + cut, :] + received(0, d, c))
    for copy in x_copies:
        copy.wait_recv()
    grad_a_out[...] = inverse_temp * (part[grp] + sib_in[0] + decode(codex_in[...], stepx_in[...]))
    for c in range(CHUNKS):
        lo = c * cut
        grad_b_out[lo : lo + cut, :] = inverse_temp * (
            home[lo : lo + cut, :] + received(1, 0, c) + received(1, 1, c)
        )

    for copy in key_copies.values():
        copy.wait_send()
    for pair in back.values():
        for copy in pair:
            copy.wait_send()
    for copy in (to_par, to_sib, onward, *pos_copies, *stat_copies, *sib_copies, *x_copies):
        copy.wait_send()


def body(view_a, view_b, positive):
    rows, width = view_a.shape
    block = rows * GROUPS
    cut = rows // CHUNKS
    lanes = -(-rows // 128) * 128
    vmem = pl.BlockSpec(memory_space=pltpu.VMEM)
    hbm = pl.BlockSpec(memory_space=pl.ANY)
    dma = pltpu.SemaphoreType.DMA
    f32, bf16, i16 = jnp.float32, jnp.bfloat16, jnp.int16
    codes = pltpu.VMEM((2, rows, width), i16)
    steps = pltpu.VMEM((2, CHUNKS, 1, width), f32)
    loss, grad_a, grad_b = pl.pallas_call(
        kernel,
        out_shape=(
            jax.ShapeDtypeStruct((1, block), f32),
            jax.ShapeDtypeStruct((rows, width), f32),
            jax.ShapeDtypeStruct((rows, width), f32),
        ),
        in_specs=[hbm, hbm, vmem],
        out_specs=(vmem, vmem, vmem),
        scratch_shapes=[
            pltpu.VMEM((GROUPS, rows, width), bf16),
            pltpu.VMEM((WINDOW, rows, width), bf16),
            pltpu.VMEM((GROUPS, 8, lanes), jnp.int32),
            pltpu.VMEM((GROUPS, 8, block), f32),
            pltpu.VMEM((WINDOW, rows, block), f32),
            pltpu.VMEM((WINDOW, rows, block), bf16),
            pltpu.VMEM((rows, block), bf16),
            pltpu.VMEM((rows, width), f32),
            pltpu.VMEM((2, rows, width), f32),
            codes, steps, codes, steps, codes, steps, codes, steps,
            pltpu.VMEM((GROUPS, rows, width), f32),
            pltpu.VMEM((2, rows, width), f32),
            pltpu.VMEM((rows, width), i16),
            pltpu.VMEM((1, width), f32),
            pltpu.VMEM((rows, width), i16),
            pltpu.VMEM((1, width), f32),
            dma((2,)),
            dma((2, 2, CHUNKS)), dma((2, 2, CHUNKS)),
            dma((3,)), dma((3,)),
            dma((3,)), dma((3,)),
            dma((3,)), dma((3,)),
            dma((2, 2, CHUNKS)), dma((2, 2, CHUNKS)),
            dma((2, 2, CHUNKS)), dma((2, 2, CHUNKS)),
            dma((2,)), dma((2,)),
            dma((2,)), dma((2,)),
        ],
        compiler_params=pltpu.CompilerParams(
            collective_id=0, has_side_effects=True, vmem_limit_bytes=56 * 2**20
        ),
        cost_estimate=pl.CostEstimate(
            flops=2 * block * rows * width * 17, bytes_accessed=rows * width * 12,
            transcendentals=2 * WINDOW * rows * block,
        ),
    )(view_a, view_b, positive.reshape(1, rows))
    row_loss = lax.dynamic_slice_in_dim(loss[0], lax.axis_index("grp") * rows, rows, 0)
    return row_loss, grad_a, grad_b


def solution(mesh):
    in_specs = (P(("blk", "grp"), None), P(("blk", "grp"), None), P(("blk", "grp")))
    out_specs = (P(("blk", "grp")), P(("blk", "grp"), None), P(("blk", "grp"), None))
    return jax.shard_map(body, mesh=mesh, in_specs=in_specs, out_specs=out_specs, check_vma=False)
```

time: 167 us -> 89.9 us (0.54)
  the two profiles are of different devices: /device:TPU:25 before, /device:TPU:8 now
where the time goes in v1:
time: 89.9 us; the launch traced here: 89.8 us
  Pallas kernels  84.8 us (94%)
  local copies, waits for them, and re-layouts  4.34 us (5%)
    pallas_call x1, Pallas kernels, body(): pl.pallas_call(kernel, out_shape=(jax.ShapeDtypeStruct((1, block), f32),...  84.8 us
    unnamed x4, local copies, waits for them, and re-layouts  3.04 us

profile of v1, /device:TPU:8, one launch (start us, length us, event | category | flops | bytes accessed | tf_op | source)
XLA Modules:
  0.0 89.8 jit_solution(9462706494172344455)
XLA Ops:
  0.6 84.8 %shard_map.58 = (f32[1,768]{1,0:T(1,128)}, f32[192,1024]{1,0:T(8,128)}, f32[192,1024]{1,0:T(8,128)}) custom-call(bf16[192,1024]{1,0:T(8,128)(2,1)} %a_in.1, bf16[192,1024]{1,0:T(8,128)(2,1)} %b_in.1, s32[1,192]{1,0:T(1,128)} %bitcast.3), custom_call_target="tpu_custom_call" | custom-call | flops 5133828096 | bytes 2359296 | tf_op jit(solution)/shard_map/pallas_call | solution.py:257
  85.4 1.3 %constant_dynamic-slice_fusion = f32[1,192]{1,0:T(1,128)} fusion(f32[1,768]{1,0:T(1,128)} %get-tuple-element.6, s32[]{:T(128)S(6)} %select_n.3), kind=kLoop, calls=%fused_computation | loop fusion | bytes 1540 | tf_op jit(solution)/shard_map/dynamic_slice | solution.py:301
  86.7 0.0 copy-start
  86.7 2.2 %copy.8 = f32[192,1024]{1,0:T(8,128)} copy(f32[192,1024]{1,0:T(8,128)} %get-tuple-element.13) | data formatting | bytes 1572864
  88.9 0.0 copy-done
  88.9 0.9 copy.9
Async XLA Ops:
  86.7 2.2 %copy-start = (f32[192,1024]{1,0:T(8,128)S(1)}, f32[192,1024]{1,0:T(8,128)}, u32[]{:S(2)}) copy-start(f32[192,1024]{1,0:T(8,128)} %get-tuple-element.14) | copy-start | bytes 2359300

commit v2 on v1

v2 whole, which is shorter than its diff:
```python
import functools

import jax
import jax.numpy as jnp
from jax import lax
from jax.experimental import pallas as pl
from jax.experimental.pallas import tpu as pltpu
from jax.sharding import PartitionSpec as P

SPAN = 2
WINDOW = 2 * SPAN + 1
GROUPS = 4
CHUNKS = 4
DETOUR = ((0, 1), (2, 3))
ORDER = (2, 3, 0, 1)
inverse_temp = 20.0
MESH = pl.DeviceIdType.MESH
TOP = 32766.0


def encode(x):
    peak = jnp.max(jnp.abs(x), axis=0, keepdims=True)
    alive = peak > 1e-30
    scale = jnp.where(alive, TOP / jnp.where(alive, peak, 1.0), 0.0)
    codes = jnp.round(x * scale).astype(jnp.int32).astype(jnp.int16)
    return codes, jnp.where(alive, peak * (1.0 / TOP), 0.0)


def decode(codes, step):
    return codes.astype(jnp.int32).astype(jnp.float32) * step


def kernel(
    a_in, b_in, pos_in, loss_out, grad_a_out, grad_b_out,
    queries, keys, pos_buf, stat_buf, scores, weights, hits_buf, home,
    code1_out, step1_out, code1_in, step1_in, code2_out, step2_out, code2_in, step2_in,
    part, sib_in, codex_out, stepx_out, codex_in, stepx_in,
    load_sem, b_send, b_recv, a_send, a_recv, p_send, p_recv, s_send, s_recv,
    c_send, c_recv, t_send, t_recv, d_send, d_recv, x_send, x_recv,
):
    rows, width = a_in.shape
    block = rows * GROUPS
    cut = rows // CHUNKS
    near = (SPAN + 1) * rows
    every = WINDOW * rows
    blk = lax.axis_index("blk")
    grp = lax.axis_index("grp")
    blocks = lax.axis_size("blk")
    right = lax.rem(blk + 1, blocks)
    left = lax.rem(blk + blocks - 1, blocks)
    sib = grp + 1 - 2 * lax.rem(grp, 2)
    par = lax.rem(grp + 2, GROUPS)
    dia = lax.rem(sib + 2, GROUPS)
    peers = (sib, par, dia)

    half = blocks // 2
    spot = lax.rem(blk, half)
    is_last, is_first = spot == half - 1, spot == 0
    is_relay = jnp.logical_or(is_last, is_first)
    detour = (is_last, is_first)
    across_x = lax.rem(blk + half, blocks)
    relay_to = lax.rem(blk + jnp.where(is_last, half + 1, half - 1), blocks)
    relay_d = jnp.where(is_last, 0, 1)

    def route(hop, d, c):
        if c not in DETOUR[hop]:
            return False, (right, left)[d]
        return detour[d], jnp.where(detour[d], across_x, (right, left)[d])

    def pick(flag, a, b):
        return b if flag is False else jnp.where(flag, a, b)

    def remote(src, dst, send, recv, to_blk, to_grp):
        return pltpu.make_async_remote_copy(
            src_ref=src, dst_ref=dst, send_sem=send, recv_sem=recv,
            device_id=(to_blk, to_grp), device_id_type=MESH,
        )

    def span(lo, size):
        return pl.ds(pl.multiple_of(lo, 16), size)

    load_b = pltpu.make_async_copy(b_in, keys.at[pl.ds(0, rows)], load_sem.at[0])
    load_a = pltpu.make_async_copy(a_in, queries.at[grp], load_sem.at[1])
    load_b.start()
    load_a.start()

    barrier = pltpu.get_barrier_semaphore()

    def greet(to_blk, to_grp):
        pl.semaphore_signal(barrier, inc=1, device_id=(to_blk, to_grp), device_id_type=MESH)

    greet(right, grp)
    greet(left, grp)
    for peer in peers:
        greet(blk, peer)

    @pl.when(is_relay)
    def _():
        greet(across_x, grp)
        greet(relay_to, grp)

    pos_buf[grp] = jnp.zeros(pos_buf.shape[1:], jnp.int32)
    pos_buf[grp, 0:1, 0:rows] = pos_in[...] - blk * block
    pl.semaphore_wait(barrier, 5 + jnp.where(is_relay, 2, 0))
    load_b.wait()

    def key_place(hop, d, c):
        if hop == 0:
            lands = rows * (1 + d) + c * cut
        else:
            lands = near + (2 * ORDER.index(c) + d) * cut
        return lands, every + hop * rows + c * cut

    def key_send(hop, d, c):
        src = c * cut if hop == 0 else rows * (1 + d) + c * cut
        direct, held = key_place(hop, d, c)
        by_relay, to_blk = route(hop, d, c)
        return remote(
            keys.at[pl.ds(src, cut)], keys.at[span(pick(by_relay, held, direct), cut)],
            b_send.at[hop, d, c], b_recv.at[hop, pick(by_relay, 2, d), c], to_blk, grp,
        )

    def key_wait(hop, d, c):
        place = keys.at[pl.ds(key_place(hop, d, c)[0], cut)]
        remote(place, place, b_send.at[hop, d, c], b_recv.at[hop, d, c], right, grp).wait_recv()

    def key_relay(hop, c):
        held = keys.at[pl.ds(key_place(hop, 0, c)[1], cut)]
        lands = jnp.where(is_last, key_place(hop, 0, c)[0], key_place(hop, 1, c)[0])
        return ((
            remote(held, held, b_send.at[hop, 2, c], b_recv.at[hop, 2, c], relay_to, grp),
            remote(held, keys.at[span(lands, cut)], b_send.at[hop, 2, c], b_recv.at[hop, relay_d, c], relay_to, grp),
        ),)

    def relay(hop, c, copies):
        if c not in DETOUR[hop]:
            return

        @pl.when(is_relay)
        def _():
            for arriving, _ in copies(hop, c):
                arriving.wait_recv()
            for _, leaving in copies(hop, c):
                leaving.start()

    key_sends = {(h, d, c): key_send(h, d, c) for h in range(2) for d in range(2) for c in range(CHUNKS)}
    middle_row = rows // 2
    query_rows = [pl.ds(i * middle_row, middle_row) for i in range(2)]
    to_par = [
        remote(queries.at[grp, r], queries.at[grp, r], a_send.at[1 + i], a_recv.at[1 + i], blk, par)
        for i, r in enumerate(query_rows)
    ]
    to_sib = remote(queries.at[grp], queries.at[grp], a_send.at[0], a_recv.at[0], blk, sib)
    for c in range(CHUNKS):
        for d in range(2):
            key_sends[0, d, c].start()
    load_a.wait()
    to_par[0].start()
    to_sib.start()

    @pl.when(jnp.logical_not(is_relay))
    def _():
        to_par[1].start()

    pos_copies = [
        remote(pos_buf.at[grp], pos_buf.at[grp], p_send.at[i], p_recv.at[i], blk, peer)
        for i, peer in enumerate(peers)
    ]
    for copy in pos_copies:
        copy.start()
    for c in range(CHUNKS):
        relay(0, c, key_relay)
    for c in ORDER:
        for d in range(2):
            key_wait(0, d, c)
            key_sends[1, d, c].start()
        if c == max(DETOUR[1]):

            @pl.when(is_relay)
            def _():
                to_par[1].start()

    onward = [
        remote(queries.at[par, r], queries.at[par, r], a_send.at[3 + i], a_recv.at[3 + i], blk, sib)
        for i, r in enumerate(query_rows)
    ]
    to_par[0].wait_recv()
    onward[0].start()
    for c in range(CHUNKS):
        relay(1, c, key_relay)
    to_par[1].wait_recv()
    onward[1].start()
    for copy in pos_copies:
        copy.wait_recv()
    place = jnp.concatenate([pos_buf[t, 0:1, 0:rows] for t in range(GROUPS)], axis=1)
    own_rows = lax.broadcasted_iota(jnp.int32, (rows, block), 0) + grp * rows
    hits = own_rows == place
    hits_buf[...] = jnp.where(hits, 1.0, 0.0).astype(jnp.bfloat16)
    to_sib.wait_recv()
    for copy in onward:
        copy.wait_recv()

    every_query = queries[...].reshape(block, width)

    def score(lo, hi):
        scores[lo:hi, :] = inverse_temp * lax.dot_general(
            keys[lo:hi, :], every_query, (((1,), (1,)), ((), ())), preferred_element_type=jnp.float32
        )
        peak = jnp.max(scores[lo:hi, :], axis=0, keepdims=True)
        return peak, jnp.sum(jnp.exp(scores[lo:hi, :] - peak), axis=0, keepdims=True)

    def merge(stats):
        peak = functools.reduce(jnp.maximum, [p for p, _ in stats])
        return peak, sum(t * jnp.exp(p - peak) for p, t in stats)

    stats = [score(0, near)]
    matched = jnp.sum(jnp.where(hits, scores[0:rows, :], 0.0), axis=0, keepdims=True)
    last = near + (CHUNKS - 1) * 2 * cut
    for c in ORDER:
        if c == ORDER[-1]:
            stats.append(score(near, last))
        for d in range(2):
            key_wait(1, d, c)
    stats.append(score(last, every))
    peak, total = merge(stats)

    stat_buf[grp, 0:1, :] = peak
    stat_buf[grp, 1:2, :] = total
    stat_buf[grp, 2:3, :] = matched
    stat_copies = [
        remote(stat_buf.at[grp], stat_buf.at[grp], s_send.at[i], s_recv.at[i], blk, peer)
        for i, peer in enumerate(peers)
    ]
    for copy in stat_copies:
        copy.start()
    for copy in stat_copies:
        copy.wait_recv()
    peak, total = merge([(stat_buf[t, 0:1, :], stat_buf[t, 1:2, :]) for t in range(GROUPS)])
    lse = peak + jnp.log(total)
    loss_out[...] = lse - sum(stat_buf[t, 2:3, :] for t in range(GROUPS))

    def weigh(lo, hi):
        weights[lo:hi, :] = jnp.exp(scores[lo:hi, :] - lse).astype(jnp.bfloat16)

    def term(lo, hi):
        weigh(lo, hi)
        return jnp.dot(weights[lo:hi, :], every_query, preferred_element_type=jnp.float32)

    code_out, step_out = (code1_out, code2_out), (step1_out, step2_out)
    code_in, step_in = (code1_in, code2_in), (step1_in, step2_in)

    def code_send(hop, d, c):
        part_rows = pl.ds(c * cut, cut)
        by_relay, to_blk = route(hop, d, c)
        slot = pick(by_relay, 2, d)
        return (
            remote(
                code_out[hop].at[d, part_rows], code_in[hop].at[slot, part_rows],
                c_send.at[hop, d, c], c_recv.at[hop, slot, c], to_blk, grp,
            ),
            remote(
                step_out[hop].at[d, c], step_in[hop].at[slot, c],
                t_send.at[hop, d, c], t_recv.at[hop, slot, c], to_blk, grp,
            ),
        )

    def code_wait(hop, d, c):
        codes, steps = code_in[hop].at[d, pl.ds(c * cut, cut)], step_in[hop].at[d, c]
        remote(codes, codes, c_send.at[hop, d, c], c_recv.at[hop, d, c], right, grp).wait_recv()
        remote(steps, steps, t_send.at[hop, d, c], t_recv.at[hop, d, c], right, grp).wait_recv()

    def code_relay(hop, c):
        part_rows = pl.ds(c * cut, cut)
        codes, steps = code_in[hop].at[2, part_rows], step_in[hop].at[2, c]
        return (
            (
                remote(codes, codes, c_send.at[hop, 2, c], c_recv.at[hop, 2, c], relay_to, grp),
                remote(codes, code_in[hop].at[relay_d, part_rows], c_send.at[hop, 2, c], c_recv.at[hop, relay_d, c], relay_to, grp),
            ),
            (
                remote(steps, steps, t_send.at[hop, 2, c], t_recv.at[hop, 2, c], relay_to, grp),
                remote(steps, step_in[hop].at[relay_d, c], t_send.at[hop, 2, c], t_recv.at[hop, relay_d, c], relay_to, grp),
            ),
        )

    code_sends = {(h, d, c): code_send(h, d, c) for h in range(2) for d in range(2) for c in range(CHUNKS)}

    def send_back(hop, d, c, value):
        codes, step = encode(value)
        code_out[hop][d, c * cut : (c + 1) * cut, :] = codes
        step_out[hop][d, c] = step
        for copy in code_sends[hop, d, c]:
            copy.start()

    def received(hop, d, c):
        code_wait(hop, d, c)
        return decode(code_in[hop][d, c * cut : (c + 1) * cut, :], step_in[hop][d, c])

    middle = near + CHUNKS // 2 * 2 * cut
    for parts, lo, hi in (((0, 1), middle, every), ((2, 3), near, middle)):
        far = term(lo, hi)
        for c in parts:
            for d in range(2):
                at = near + (2 * ORDER.index(c) + 1 - d) * cut - lo
                send_back(0, d, c, far[at : at + cut, :])
    weigh(0, near)

    across = (((0,), (0,)), ((), ()))
    pair = GROUPS // 2

    def query_part(chip):
        lanes = pl.ds(pl.multiple_of(chip * pair * rows, 128), pair * rows)
        value = lax.dot_general(weights[:, lanes], keys[0:every, :], across, preferred_element_type=jnp.float32)
        value = value - lax.dot_general(
            hits_buf[:, lanes], keys[0:rows, :], across, preferred_element_type=jnp.float32
        )
        part[pl.ds(chip * pair, pair)] = value.reshape(pair, rows, width)

    chip = grp // pair
    sib_copies = [
        remote(part.at[t], sib_in.at[i], d_send.at[i], d_recv.at[i], blk, sib)
        for i, t in ((0, sib), (1, dia))
    ]
    query_part(1 - chip)
    sib_copies[1].start()
    query_part(chip)
    sib_copies[0].start()
    sib_copies[1].wait_recv()
    x_copies = []
    for i, r in enumerate(query_rows):
        codes, step = encode(part[par, r] + sib_in[1, r])
        codex_out[r, :] = codes
        stepx_out[i] = step
        x_copies.append((
            remote(codex_out.at[r], codex_in.at[r], x_send.at[0, i], x_recv.at[0, i], blk, par),
            remote(stepx_out.at[i], stepx_in.at[i], x_send.at[1, i], x_recv.at[1, i], blk, par),
        ))
    for copy in x_copies[0]:
        copy.start()

    for c in range(CHUNKS):
        relay(0, c, code_relay)
    home[...] = jnp.dot(weights[0:near, :], every_query, preferred_element_type=jnp.float32)
    home[0:rows, :] -= jnp.dot(hits_buf[...], every_query, preferred_element_type=jnp.float32)
    for c in ORDER:
        for d in range(2):
            lo = rows * (2 - d) + c * cut
            send_back(1, d, c, home[lo : lo + cut, :] + received(0, d, c))
        if c == max(DETOUR[1]):
            for copy in x_copies[1]:
                copy.start()

    for c in range(CHUNKS):
        relay(1, c, code_relay)
    for c in ORDER:
        lo = c * cut
        grad_b_out[lo : lo + cut, :] = inverse_temp * (
            home[lo : lo + cut, :] + received(1, 0, c) + received(1, 1, c)
        )
        if c == ORDER[1]:
            sib_copies[0].wait_recv()
            for i, r in enumerate(query_rows):
                for copy in x_copies[i]:
                    copy.wait_recv()
                grad_a_out[r, :] = inverse_temp * (
                    part[grp, r] + sib_in[0, r] + decode(codex_in[r, :], stepx_in[i])
                )

    for copy in key_sends.values():
        copy.wait_send()
    for pair in code_sends.values():
        for copy in pair:
            copy.wait_send()
    for copy in (*to_par, to_sib, *onward, *pos_copies, *stat_copies, *sib_copies, *x_copies[0], *x_copies[1]):
        copy.wait_send()

    @pl.when(is_relay)
    def _():
        for hop in range(2):
            for c in DETOUR[hop]:
                for _, leaving in (*key_relay(hop, c), *code_relay(hop, c)):
                    leaving.wait_send()


def body(view_a, view_b, positive):
    rows, width = view_a.shape
    block = rows * GROUPS
    lanes = -(-rows // 128) * 128
    vmem = pl.BlockSpec(memory_space=pltpu.VMEM)
    hbm = pl.BlockSpec(memory_space=pl.ANY)
    dma = pltpu.SemaphoreType.DMA
    f32, bf16, i16 = jnp.float32, jnp.bfloat16, jnp.int16
    codes_out, steps_out = pltpu.VMEM((2, rows, width), i16), pltpu.VMEM((2, CHUNKS, 1, width), f32)
    codes_in, steps_in = pltpu.VMEM((3, rows, width), i16), pltpu.VMEM((3, CHUNKS, 1, width), f32)
    loss, grad_a, grad_b = pl.pallas_call(
        kernel,
        out_shape=(
            jax.ShapeDtypeStruct((1, block), f32),
            jax.ShapeDtypeStruct((rows, width), f32),
            jax.ShapeDtypeStruct((rows, width), f32),
        ),
        in_specs=[hbm, hbm, vmem],
        out_specs=(vmem, vmem, vmem),
        scratch_shapes=[
            pltpu.VMEM((GROUPS, rows, width), bf16),
            pltpu.VMEM(((WINDOW + 2) * rows, width), bf16),
            pltpu.VMEM((GROUPS, 8, lanes), jnp.int32),
            pltpu.VMEM((GROUPS, 8, block), f32),
            pltpu.VMEM((WINDOW * rows, block), f32),
            pltpu.VMEM((WINDOW * rows, block), bf16),
            pltpu.VMEM((rows, block), bf16),
            pltpu.VMEM(((SPAN + 1) * rows, width), f32),
            codes_out, steps_out, codes_in, steps_in, codes_out, steps_out, codes_in, steps_in,
            pltpu.VMEM((GROUPS, rows, width), f32),
            pltpu.VMEM((2, rows, width), f32),
            pltpu.VMEM((rows, width), i16),
            pltpu.VMEM((2, 1, width), f32),
            pltpu.VMEM((rows, width), i16),
            pltpu.VMEM((2, 1, width), f32),
            dma((2,)),
            dma((2, 3, CHUNKS)), dma((2, 3, CHUNKS)),
            dma((5,)), dma((5,)),
            dma((3,)), dma((3,)),
            dma((3,)), dma((3,)),
            dma((2, 3, CHUNKS)), dma((2, 3, CHUNKS)),
            dma((2, 3, CHUNKS)), dma((2, 3, CHUNKS)),
            dma((2,)), dma((2,)),
            dma((2, 2)), dma((2, 2)),
        ],
        compiler_params=pltpu.CompilerParams(
            collective_id=0, has_side_effects=True, vmem_limit_bytes=56 * 2**20
        ),
        cost_estimate=pl.CostEstimate(
            flops=2 * block * rows * width * 17, bytes_accessed=rows * width * 12,
            transcendentals=2 * WINDOW * rows * block,
        ),
    )(view_a, view_b, positive.reshape(1, rows))
    row_loss = lax.dynamic_slice_in_dim(loss[0], lax.axis_index("grp") * rows, rows, 0)
    return row_loss, grad_a, grad_b


def solution(mesh):
    in_specs = (P(("blk", "grp"), None), P(("blk", "grp"), None), P(("blk", "grp")))
    out_specs = (P(("blk", "grp")), P(("blk", "grp"), None), P(("blk", "grp"), None))
    return jax.shard_map(body, mesh=mesh, in_specs=in_specs, out_specs=out_specs, check_vma=False)
```

time: 89.9 us -> 74.3 us (0.83)
  the two profiles are of different devices: /device:TPU:8 before, /device:TPU:1 now
where the time goes in v2:
time: 74.3 us; the launch traced here: 74.1 us
  Pallas kernels  69.1 us (93%)
  local copies, waits for them, and re-layouts  4.34 us (6%)
    pallas_call x1, Pallas kernels, body(): pl.pallas_call(kernel, out_shape=(jax.ShapeDtypeStruct((1, block), f32),...  69.1 us
    unnamed x4, local copies, waits for them, and re-layouts  3.04 us

profile of v2, /device:TPU:1, one launch (start us, length us, event | category | flops | bytes accessed | tf_op | source)
XLA Modules:
  0.0 74.1 jit_solution(11156137122220459944)
XLA Ops:
  0.6 69.1 %shard_map.58 = (f32[1,768]{1,0:T(1,128)}, f32[192,1024]{1,0:T(8,128)}, f32[192,1024]{1,0:T(8,128)}) custom-call(bf16[192,1024]{1,0:T(8,128)(2,1)} %a_in.1, bf16[192,1024]{1,0:T(8,128)(2,1)} %b_in.1, s32[1,192]{1,0:T(1,128)} %bitcast.3), custom_call_target="tpu_custom_call" | custom-call | flops 5133828096 | bytes 2359296 | tf_op jit(solution)/shard_map/pallas_call | solution.py:395
  69.7 1.3 %constant_dynamic-slice_fusion = f32[1,192]{1,0:T(1,128)} fusion(f32[1,768]{1,0:T(1,128)} %get-tuple-element.6, s32[]{:T(128)S(6)} %select_n.3), kind=kLoop, calls=%fused_computation | loop fusion | bytes 1540 | tf_op jit(solution)/shard_map/dynamic_slice | solution.py:438
  71.0 0.0 copy-start
  71.0 2.2 %copy.8 = f32[192,1024]{1,0:T(8,128)} copy(f32[192,1024]{1,0:T(8,128)} %get-tuple-element.13) | data formatting | bytes 1572864
  73.2 0.0 copy-done
  73.2 0.9 %copy.9 = f32[192,1024]{1,0:T(8,128)} copy(f32[192,1024]{1,0:T(8,128)S(1)} %copy-done) | data formatting | bytes 1572864
Async XLA Ops:
  71.0 2.2 %copy-start = (f32[192,1024]{1,0:T(8,128)S(1)}, f32[192,1024]{1,0:T(8,128)}, u32[]{:S(2)}) copy-start(f32[192,1024]{1,0:T(8,128)} %get-tuple-element.14) | copy-start | bytes 2359300

commit v3 on v2

--- a/solution.py
+++ b/solution.py
@@ -237,7 +237,11 @@
         copy.wait_recv()
     peak, total = merge([(stat_buf[t, 0:1, :], stat_buf[t, 1:2, :]) for t in range(GROUPS)])
     lse = peak + jnp.log(total)
-    loss_out[...] = lse - sum(stat_buf[t, 2:3, :] for t in range(GROUPS))
+    losses = lse - sum(stat_buf[t, 2:3, :] for t in range(GROUPS))
+    own_loss = losses[:, 0:rows]
+    for t in range(1, GROUPS):
+        own_loss = jnp.where(grp == t, losses[:, t * rows : (t + 1) * rows], own_loss)
+    loss_out[...] = own_loss
 
     def weigh(lo, hi):
         weights[lo:hi, :] = jnp.exp(scores[lo:hi, :] - lse).astype(jnp.bfloat16)
@@ -338,6 +342,11 @@
     for copy in x_copies[0]:
         copy.start()
 
+    @pl.when(jnp.logical_not(is_relay))
+    def _():
+        for copy in x_copies[1]:
+            copy.start()
+
     for c in range(CHUNKS):
         relay(0, c, code_relay)
     home[...] = jnp.dot(weights[0:near, :], every_query, preferred_element_type=jnp.float32)
@@ -347,24 +356,23 @@
             lo = rows * (2 - d) + c * cut
             send_back(1, d, c, home[lo : lo + cut, :] + received(0, d, c))
         if c == max(DETOUR[1]):
-            for copy in x_copies[1]:
-                copy.start()
+
+            @pl.when(is_relay)
+            def _():
+                for copy in x_copies[1]:
+                    copy.start()
 
     for c in range(CHUNKS):
         relay(1, c, code_relay)
     for c in ORDER:
         lo = c * cut
-        grad_b_out[lo : lo + cut, :] = inverse_temp * (
-            home[lo : lo + cut, :] + received(1, 0, c) + received(1, 1, c)
-        )
+        grad_b_out[lo : lo + cut, :] = home[lo : lo + cut, :] + received(1, 0, c) + received(1, 1, c)
         if c == ORDER[1]:
             sib_copies[0].wait_recv()
             for i, r in enumerate(query_rows):
                 for copy in x_copies[i]:
                     copy.wait_recv()
-                grad_a_out[r, :] = inverse_temp * (
-                    part[grp, r] + sib_in[0, r] + decode(codex_in[r, :], stepx_in[i])
-                )
+                grad_a_out[r, :] = part[grp, r] + sib_in[0, r] + decode(codex_in[r, :], stepx_in[i])
 
     for copy in key_sends.values():
         copy.wait_send()
@@ -395,9 +403,9 @@
     loss, grad_a, grad_b = pl.pallas_call(
         kernel,
         out_shape=(
-            jax.ShapeDtypeStruct((1, block), f32),
-            jax.ShapeDtypeStruct((rows, width), f32),
-            jax.ShapeDtypeStruct((rows, width), f32),
+            pltpu.VMEM((1, rows), f32),
+            pltpu.VMEM((rows, width), f32),
+            pltpu.VMEM((rows, width), f32),
         ),
         in_specs=[hbm, hbm, vmem],
         out_specs=(vmem, vmem, vmem),
@@ -428,15 +436,14 @@
             dma((2, 2)), dma((2, 2)),
         ],
         compiler_params=pltpu.CompilerParams(
-            collective_id=0, has_side_effects=True, vmem_limit_bytes=56 * 2**20
+            collective_id=0, has_side_effects=True, vmem_limit_bytes=53 * 2**20
         ),
         cost_estimate=pl.CostEstimate(
             flops=2 * block * rows * width * 17, bytes_accessed=rows * width * 12,
             transcendentals=2 * WINDOW * rows * block,
         ),
     )(view_a, view_b, positive.reshape(1, rows))
-    row_loss = lax.dynamic_slice_in_dim(loss[0], lax.axis_index("grp") * rows, rows, 0)
-    return row_loss, grad_a, grad_b
+    return loss.reshape(rows), inverse_temp * grad_a, inverse_temp * grad_b
 
 
 def solution(mesh):

time: 74.3 us -> 70.6 us (0.950)
  local copies, waits for them, and re-layouts: 4.34 us -> 0.56 us
  other arithmetic: 0 us -> 1.34 us
  Pallas kernels: 69.1 us -> 67.9 us
    unnamed x4 -> x1, local copies, waits for them, and re-layouts: 3.04 us -> 0.56 us
    mul x0 -> x1, other arithmetic: none -> 1.34 us  [body(): return (loss.reshape(rows), inverse_temp * grad_a, inverse_temp * grad_b)]
    dynamic_slice x1 -> x0, local copies, waits for them, and re-layouts: 1.3 us -> none  [body(): lax.dynamic_slice_in_dim(loss[0], lax.axis_index('grp') * rows, rows, 0)]
    pallas_call x1, Pallas kernels: 69.1 us -> 67.9 us  [body(): pl.pallas_call(kernel, out_shape=(pltpu.VMEM((1, rows), f32), pltpu.VMEM(...]
where the time goes in v3:
time: 70.6 us; the launch traced here: 70.4 us
  Pallas kernels  67.9 us (96%)
  other arithmetic  1.34 us (2%)
    pallas_call x1, Pallas kernels, body(): pl.pallas_call(kernel, out_shape=(pltpu.VMEM((1, rows), f32), pltpu.VMEM(...  67.9 us

profile of v3, /device:TPU:1, one launch (start us, length us, event | category | flops | bytes accessed | tf_op | source)
XLA Modules:
  0.0 70.4 jit_solution(422213313678793455)
XLA Ops:
  0.6 67.9 %shard_map.58 = (f32[1,192]{1,0:T(1,128)S(1)}, f32[192,1024]{1,0:T(8,128)S(1)}, f32[192,1024]{1,0:T(8,128)S(1)}) custom-call(bf16[192,1024]{1,0:T(8,128)(2,1)} %a_in.1, bf16[192,1024]{1,0:T(8,128)(2,1)} %b_in.1, s32[1,192]{1,0:T(1,128)} %bitcast.3), custom_call_target="tpu_custom_call" | custom-call | flops 5133828096 | bytes 2359296 | tf_op jit(solution)/shard_map/pallas_call | solution.py:403
  68.5 0.6 copy.7
  69.1 1.3 %broadcast_multiply_fusion = (f32[192,1024]{1,0:T(8,128)}, f32[192,1024]{1,0:T(8,128)}) fusion(f32[192,1024]{1,0:T(8,128)S(1)} %get-tuple-element.8, f32[192,1024]{1,0:T(8,128)S(1)} %get-tuple-element.7), kind=kLoop, calls=%fused_computation | loop fusion | flops 393216 | bytes 3145728 | tf_op jit(solution)/shard_map/mul | solution.py:446

commit v4 on v3

--- a/solution.py
+++ b/solution.py
@@ -11,8 +11,8 @@
 WINDOW = 2 * SPAN + 1
 GROUPS = 4
 CHUNKS = 4
-DETOUR = ((0, 1), (2, 3))
-ORDER = (2, 3, 0, 1)
+KEY_DETOUR = ((0, 1), (0,))
+CODE_DETOUR = ((0,), (0, 1))
 inverse_temp = 20.0
 MESH = pl.DeviceIdType.MESH
 TOP = 32766.0
@@ -62,8 +62,8 @@
     relay_to = lax.rem(blk + jnp.where(is_last, half + 1, half - 1), blocks)
     relay_d = jnp.where(is_last, 0, 1)
 
-    def route(hop, d, c):
-        if c not in DETOUR[hop]:
+    def route(detours, d, c):
+        if c not in detours:
             return False, (right, left)[d]
         return detour[d], jnp.where(detour[d], across_x, (right, left)[d])
 
@@ -108,13 +108,13 @@
         if hop == 0:
             lands = rows * (1 + d) + c * cut
         else:
-            lands = near + (2 * ORDER.index(c) + d) * cut
+            lands = near + (2 * c + d) * cut
         return lands, every + hop * rows + c * cut
 
     def key_send(hop, d, c):
         src = c * cut if hop == 0 else rows * (1 + d) + c * cut
         direct, held = key_place(hop, d, c)
-        by_relay, to_blk = route(hop, d, c)
+        by_relay, to_blk = route(KEY_DETOUR[hop], d, c)
         return remote(
             keys.at[pl.ds(src, cut)], keys.at[span(pick(by_relay, held, direct), cut)],
             b_send.at[hop, d, c], b_recv.at[hop, pick(by_relay, 2, d), c], to_blk, grp,
@@ -133,9 +133,6 @@
         ),)
 
     def relay(hop, c, copies):
-        if c not in DETOUR[hop]:
-            return
-
         @pl.when(is_relay)
         def _():
             for arriving, _ in copies(hop, c):
@@ -155,12 +152,12 @@
         for d in range(2):
             key_sends[0, d, c].start()
     load_a.wait()
-    to_par[0].start()
     to_sib.start()
 
     @pl.when(jnp.logical_not(is_relay))
     def _():
-        to_par[1].start()
+        for copy in to_par:
+            copy.start()
 
     pos_copies = [
         remote(pos_buf.at[grp], pos_buf.at[grp], p_send.at[i], p_recv.at[i], blk, peer)
@@ -168,37 +165,77 @@
     ]
     for copy in pos_copies:
         copy.start()
-    for c in range(CHUNKS):
-        relay(0, c, key_relay)
-    for c in ORDER:
-        for d in range(2):
-            key_wait(0, d, c)
-            key_sends[1, d, c].start()
-        if c == max(DETOUR[1]):
-
-            @pl.when(is_relay)
-            def _():
-                to_par[1].start()
+
+    def take(d, c):
+        key_wait(0, d, c)
+        key_sends[1, d, c].start()
+
+    def take_at_edge(inner):
+        for c in KEY_DETOUR[0]:
+            take(inner, c)
+            for arriving, leaving in key_relay(0, c):
+                arriving.wait_recv()
+                leaving.start()
+        for copy in to_par:
+            copy.start()
+        direct = [c for c in range(CHUNKS) if c not in KEY_DETOUR[0]]
+        for d, parts in ((inner, direct), (1 - inner, direct), (1 - inner, KEY_DETOUR[0])):
+            for c in parts:
+                take(d, c)
+        for c in KEY_DETOUR[1]:
+            for arriving, leaving in key_relay(1, c):
+                arriving.wait_recv()
+                leaving.start()
+
+    @pl.when(is_last)
+    def _():
+        take_at_edge(0)
+
+    @pl.when(is_first)
+    def _():
+        take_at_edge(1)
+
+    @pl.when(jnp.logical_not(is_relay))
+    def _():
+        for c in range(CHUNKS):
+            for d in range(2):
+                take(d, c)
 
     onward = [
         remote(queries.at[par, r], queries.at[par, r], a_send.at[3 + i], a_recv.at[3 + i], blk, sib)
         for i, r in enumerate(query_rows)
     ]
-    to_par[0].wait_recv()
-    onward[0].start()
-    for c in range(CHUNKS):
-        relay(1, c, key_relay)
-    to_par[1].wait_recv()
-    onward[1].start()
     for copy in pos_copies:
         copy.wait_recv()
     place = jnp.concatenate([pos_buf[t, 0:1, 0:rows] for t in range(GROUPS)], axis=1)
     own_rows = lax.broadcasted_iota(jnp.int32, (rows, block), 0) + grp * rows
     hits = own_rows == place
     hits_buf[...] = jnp.where(hits, 1.0, 0.0).astype(jnp.bfloat16)
+    pair = GROUPS // 2
+    chip = grp // pair
+
+    def lanes_of(chip):
+        return pl.ds(pl.multiple_of(chip * pair * rows, 128), pair * rows)
+
+    def score_near(chip):
+        lanes = lanes_of(chip)
+        value = inverse_temp * lax.dot_general(
+            keys[0:near, :], queries[pl.ds(chip * pair, pair)].reshape(pair * rows, width),
+            (((1,), (1,)), ((), ())), preferred_element_type=jnp.float32,
+        )
+        scores[0:near, lanes] = value
+        peak = jnp.max(value, axis=0, keepdims=True)
+        stat_buf[grp, 3:4, lanes] = peak
+        stat_buf[grp, 4:5, lanes] = jnp.sum(jnp.exp(value - peak), axis=0, keepdims=True)
+
     to_sib.wait_recv()
+    score_near(chip)
+    for i in range(2):
+        to_par[i].wait_recv()
+        onward[i].start()
     for copy in onward:
         copy.wait_recv()
+    score_near(1 - chip)
 
     every_query = queries[...].reshape(block, width)
 
@@ -213,11 +250,11 @@
         peak = functools.reduce(jnp.maximum, [p for p, _ in stats])
         return peak, sum(t * jnp.exp(p - peak) for p, t in stats)
 
-    stats = [score(0, near)]
+    stats = [(stat_buf[grp, 3:4, :], stat_buf[grp, 4:5, :])]
     matched = jnp.sum(jnp.where(hits, scores[0:rows, :], 0.0), axis=0, keepdims=True)
     last = near + (CHUNKS - 1) * 2 * cut
-    for c in ORDER:
-        if c == ORDER[-1]:
+    for c in range(CHUNKS):
+        if c == CHUNKS - 1:
             stats.append(score(near, last))
         for d in range(2):
             key_wait(1, d, c)
@@ -255,7 +292,7 @@
 
     def code_send(hop, d, c):
         part_rows = pl.ds(c * cut, cut)
-        by_relay, to_blk = route(hop, d, c)
+        by_relay, to_blk = route(CODE_DETOUR[hop], d, c)
         slot = pick(by_relay, 2, d)
         return (
             remote(
@@ -301,26 +338,23 @@
         return decode(code_in[hop][d, c * cut : (c + 1) * cut, :], step_in[hop][d, c])
 
     middle = near + CHUNKS // 2 * 2 * cut
-    for parts, lo, hi in (((0, 1), middle, every), ((2, 3), near, middle)):
+    for parts, lo, hi in (((0, 1), near, middle), ((2, 3), middle, every)):
         far = term(lo, hi)
         for c in parts:
             for d in range(2):
-                at = near + (2 * ORDER.index(c) + 1 - d) * cut - lo
+                at = near + (2 * c + 1 - d) * cut - lo
                 send_back(0, d, c, far[at : at + cut, :])
     weigh(0, near)
 
     across = (((0,), (0,)), ((), ()))
-    pair = GROUPS // 2
-
     def query_part(chip):
-        lanes = pl.ds(pl.multiple_of(chip * pair * rows, 128), pair * rows)
+        lanes = lanes_of(chip)
         value = lax.dot_general(weights[:, lanes], keys[0:every, :], across, preferred_element_type=jnp.float32)
         value = value - lax.dot_general(
             hits_buf[:, lanes], keys[0:rows, :], across, preferred_element_type=jnp.float32
         )
         part[pl.ds(chip * pair, pair)] = value.reshape(pair, rows, width)
 
-    chip = grp // pair
     sib_copies = [
         remote(part.at[t], sib_in.at[i], d_send.at[i], d_recv.at[i], blk, sib)
         for i, t in ((0, sib), (1, dia))
@@ -347,27 +381,43 @@
         for copy in x_copies[1]:
             copy.start()
 
-    for c in range(CHUNKS):
+    for c in CODE_DETOUR[0]:
         relay(0, c, code_relay)
     home[...] = jnp.dot(weights[0:near, :], every_query, preferred_element_type=jnp.float32)
     home[0:rows, :] -= jnp.dot(hits_buf[...], every_query, preferred_element_type=jnp.float32)
-    for c in ORDER:
-        for d in range(2):
-            lo = rows * (2 - d) + c * cut
-            send_back(1, d, c, home[lo : lo + cut, :] + received(0, d, c))
-        if c == max(DETOUR[1]):
-
-            @pl.when(is_relay)
-            def _():
+    def pass_home(d, c):
+        lo = rows * (2 - d) + c * cut
+        send_back(1, d, c, home[lo : lo + cut, :] + received(0, d, c))
+
+    def pass_at_edge(inner):
+        for c in range(CHUNKS):
+            pass_home(inner, c)
+            if c == max(CODE_DETOUR[1]):
                 for copy in x_copies[1]:
                     copy.start()
-
+        for c in (2, 3, 0, 1):
+            pass_home(1 - inner, c)
+
+    @pl.when(is_last)
+    def _():
+        pass_at_edge(0)
+
+    @pl.when(is_first)
+    def _():
+        pass_at_edge(1)
+
+    @pl.when(jnp.logical_not(is_relay))
+    def _():
+        for c in range(CHUNKS):
+            for d in range(2):
+                pass_home(d, c)
+
+    for c in CODE_DETOUR[1]:
+        relay(1, c, code_relay)
     for c in range(CHUNKS):
-        relay(1, c, code_relay)
-    for c in ORDER:
         lo = c * cut
         grad_b_out[lo : lo + cut, :] = home[lo : lo + cut, :] + received(1, 0, c) + received(1, 1, c)
-        if c == ORDER[1]:
+        if c == 1:
             sib_copies[0].wait_recv()
             for i, r in enumerate(query_rows):
                 for copy in x_copies[i]:
@@ -385,8 +435,11 @@
     @pl.when(is_relay)
     def _():
         for hop in range(2):
-            for c in DETOUR[hop]:
-                for _, leaving in (*key_relay(hop, c), *code_relay(hop, c)):
+            for c in KEY_DETOUR[hop]:
+                for _, leaving in key_relay(hop, c):
+                    leaving.wait_send()
+            for c in CODE_DETOUR[hop]:
+                for _, leaving in code_relay(hop, c):
                     leaving.wait_send()
 
 

time: 70.6 us -> 68.6 us (0.972); the launches traced: 70.4 us -> 67.4 us
  Pallas kernels: 67.9 us -> 64.9 us
    pallas_call x1, Pallas kernels: 67.9 us -> 64.9 us  [body(): pl.pallas_call(kernel, out_shape=(pltpu.VMEM((1, rows), f32), pltpu.VMEM(...]
where the time goes in v4:
time: 68.6 us; the launch traced here: 67.4 us
  Pallas kernels  64.9 us (95%)
  other arithmetic  1.34 us (2%)
    pallas_call x1, Pallas kernels, body(): pl.pallas_call(kernel, out_shape=(pltpu.VMEM((1, rows), f32), pltpu.VMEM(...  64.9 us

profile of v4, /device:TPU:1, one launch (start us, length us, event | category | flops | bytes accessed | tf_op | source)
XLA Modules:
  0.0 67.4 jit_solution(13700848385537567699)
XLA Ops:
  0.6 64.9 %shard_map.58 = (f32[1,192]{1,0:T(1,128)S(1)}, f32[192,1024]{1,0:T(8,128)S(1)}, f32[192,1024]{1,0:T(8,128)S(1)}) custom-call(bf16[192,1024]{1,0:T(8,128)(2,1)} %a_in.1, bf16[192,1024]{1,0:T(8,128)(2,1)} %b_in.1, s32[1,192]{1,0:T(1,128)} %bitcast.3), custom_call_target="tpu_custom_call" | custom-call | flops 5133828096 | bytes 2359296 | tf_op jit(solution)/shard_map/pallas_call | solution.py:456
  65.5 0.6 copy.7
  66.1 1.3 %broadcast_multiply_fusion = (f32[192,1024]{1,0:T(8,128)}, f32[192,1024]{1,0:T(8,128)}) fusion(f32[192,1024]{1,0:T(8,128)S(1)} %get-tuple-element.8, f32[192,1024]{1,0:T(8,128)S(1)} %get-tuple-element.7), kind=kLoop, calls=%fused_computation | loop fusion | flops 393216 | bytes 3145728 | tf_op jit(solution)/shard_map/mul | solution.py:499

commit v5 on v4

--- a/solution.py
+++ b/solution.py
@@ -11,7 +11,7 @@
 WINDOW = 2 * SPAN + 1
 GROUPS = 4
 CHUNKS = 4
-KEY_DETOUR = ((0, 1), (0,))
+KEY_DETOUR = ((0, 1), (0, 1))
 CODE_DETOUR = ((0,), (0, 1))
 inverse_temp = 20.0
 MESH = pl.DeviceIdType.MESH

time: 68.6 us -> 68.8 us (level); the launches traced: 67.4 us -> 68.7 us
  Pallas kernels: 64.9 us -> 66.1 us
    pallas_call x1, Pallas kernels: 64.9 us -> 66.1 us  [body(): pl.pallas_call(kernel, out_shape=(pltpu.VMEM((1, rows), f32), pltpu.VMEM(...]
where the time goes in v5:
time: 68.8 us; the launch traced here: 68.7 us
  Pallas kernels  66.1 us (96%)
  other arithmetic  1.34 us (2%)
    pallas_call x1, Pallas kernels, body(): pl.pallas_call(kernel, out_shape=(pltpu.VMEM((1, rows), f32), pltpu.VMEM(...  66.1 us

profile of v5, /device:TPU:1, one launch (start us, length us, event | category | flops | bytes accessed | tf_op | source)
XLA Modules:
  0.0 68.7 jit_solution(8222481794037783217)
XLA Ops:
  0.6 66.1 %shard_map.58 = (f32[1,192]{1,0:T(1,128)S(1)}, f32[192,1024]{1,0:T(8,128)S(1)}, f32[192,1024]{1,0:T(8,128)S(1)}) custom-call(bf16[192,1024]{1,0:T(8,128)(2,1)} %a_in.1, bf16[192,1024]{1,0:T(8,128)(2,1)} %b_in.1, s32[1,192]{1,0:T(1,128)} %bitcast.3), custom_call_target="tpu_custom_call" | custom-call | flops 5133828096 | bytes 2359296 | tf_op jit(solution)/shard_map/pallas_call | solution.py:456
  66.8 0.6 copy.7
  67.3 1.3 %broadcast_multiply_fusion = (f32[192,1024]{1,0:T(8,128)}, f32[192,1024]{1,0:T(8,128)}) fusion(f32[192,1024]{1,0:T(8,128)S(1)} %get-tuple-element.8, f32[192,1024]{1,0:T(8,128)S(1)} %get-tuple-element.7), kind=kLoop, calls=%fused_computation | loop fusion | flops 393216 | bytes 3145728 | tf_op jit(solution)/shard_map/mul | solution.py:499
